TPU v7x, 32 devices: a whole 2x2x4 slice. The times are simulated.
32 devices in a mesh: chan: 8 (over y, x, core), beam: 4 (over z).
Axes of the slice: x: 2, y: 2, z: 4, core: 2. Of those that a mesh axis runs over, the one named last changes fastest.
Arguments:
- images: float32 [256, 36, 128, 128], P('chan', 'beam')
- beam_weight: float32 [36, 128, 128], P('beam'), may hold values from 0.2 to 1
- offsets: int32 [36, 2], P('beam'), may hold values from 0 to 384, as said below
- rejected_indicator: int32 [256, 192, 512], P('chan', None, 'beam'), may hold values 0 or 1
- regression_indicator: int32 [256], replicated, may hold values 0 or 1
Outputs:
- cleaned_cube: float32 [256, 192, 512], P(None, 'chan', 'beam')
Inputs may be any that keep to these rules, and one draw needn't show every extreme that they name: `offsets`: beam b = 6 r + q sits near row r * 64 // 5 and column q * 384 // 5, within 16; every sky pixel is covered by some beam; the first and last row and column of beams lie at the field's edges.
All inputs are finite; a program needn't handle non-finite values. No bound on the sum of `rejected_indicator` on one device may be relied on, other than what follows from the above.
Results may differ from a plain program's by a relative error of at most 0.00023.
Values sent between devices are 32-bit elements; how exact they have to be, the bound alone decides.
A program may use at most 128 MiB of HBM per device.

v0:
```python
import jax
import jax.numpy as jnp
from jax import lax
from jax.sharding import PartitionSpec as P

MOS_ROWS = 192
MOS_COLS = 512


def legendre(count):
    position = (2.0 * jnp.arange(count).astype(jnp.float32) + 1.0) / count - 1.0
    square = position * position
    return jnp.stack(
        [
            jnp.ones_like(position),
            position,
            0.5 * (3.0 * square - 1.0),
            0.5 * (5.0 * square * position - 3.0 * position),
        ],
        axis=1,
    )


def solve_cubic(normal_matrix, right_side):
    factor = {}
    for outer in range(4):
        for inner in range(outer + 1):
            value = normal_matrix[outer * 4 + inner]
            for other in range(inner):
                value = value - factor[outer, other] * factor[inner, other]
            if outer == inner:
                factor[outer, outer] = jnp.sqrt(value)
            else:
                factor[outer, inner] = value / factor[inner, inner]
    forward = []
    for outer in range(4):
        value = right_side[outer]
        for other in range(outer):
            value = value - factor[outer, other] * forward[other]
        forward.append(value / factor[outer, outer])
    backward = [None] * 4
    for outer in range(3, -1, -1):
        value = forward[outer]
        for other in range(outer + 1, 4):
            value = value - factor[other, outer] * backward[other]
        backward[outer] = value / factor[outer, outer]
    return jnp.stack(backward, axis=0)


def clean_pair(pair):
    sky_tile, weight_tile = pair
    channels, rows, columns = sky_tile.shape
    celestial_image = sky_tile.reshape(channels, rows * columns)
    importance_factor = weight_tile.reshape(channels, rows * columns)
    table = legendre(channels)
    products = jnp.stack(
        [table[:, outer] * table[:, inner] for outer in range(4) for inner in range(4)], axis=0
    )
    normal_matrix = jnp.dot(
        products,
        importance_factor,
        precision=lax.Precision.HIGHEST,
        preferred_element_type=jnp.float32,
    )
    right_side = jnp.dot(
        table.T,
        importance_factor * celestial_image,
        precision=lax.Precision.HIGHEST,
        preferred_element_type=jnp.float32,
    )
    coefficients = solve_cubic(normal_matrix, right_side)
    continuum = jnp.dot(
        table, coefficients, precision=lax.Precision.HIGHEST, preferred_element_type=jnp.float32
    )
    residual = celestial_image - continuum
    padded = jnp.pad(residual, ((1, 1), (0, 0)))
    smoothed = 0.25 * padded[:-2] + 0.5 * residual + 0.25 * padded[2:]
    return smoothed.reshape(channels, rows, columns)


def local(images, beam_weight, offsets, rejected_indicator, regression_indicator):
    ch_dev = images.shape[0]
    beam_dev = images.shape[1]
    side = images.shape[2]
    all_channels = regression_indicator.shape[0]
    first_channel = lax.axis_index("chan") * ch_dev
    channel_ids = first_channel + jnp.arange(ch_dev, dtype=jnp.int32)
    exponent = 1.0 + 0.5 * channel_ids.astype(jnp.float32) / (all_channels - 1)
    empty = jnp.zeros((ch_dev, MOS_ROWS, MOS_COLS), jnp.float32)

    def place(index, state_pair):
        dividend_accumulator, normalizer_accumulated = state_pair
        beam_image = lax.dynamic_index_in_dim(images, index, 1, keepdims=False)
        log_weight = jnp.log(lax.dynamic_index_in_dim(beam_weight, index, 0, keepdims=False))
        response = jnp.exp(exponent[:, None, None] * log_weight[None])
        corner = (jnp.zeros((), jnp.int32), offsets[index, 0], offsets[index, 1])
        extent = (ch_dev, side, side)
        dividend_accumulator = lax.dynamic_update_slice(
            dividend_accumulator,
            lax.dynamic_slice(dividend_accumulator, corner, extent) + response * beam_image,
            corner,
        )
        normalizer_accumulated = lax.dynamic_update_slice(
            normalizer_accumulated,
            lax.dynamic_slice(normalizer_accumulated, corner, extent) + response * response,
            corner,
        )
        return (dividend_accumulator, normalizer_accumulated)

    dividend_accumulator, normalizer_accumulated = lax.fori_loop(0, beam_dev, place, (empty, empty))
    dividend_accumulator, normalizer_accumulated = (
        lax.psum_scatter(dividend_accumulator, "beam", scatter_dimension=2, tiled=True),
        lax.psum_scatter(normalizer_accumulated, "beam", scatter_dimension=2, tiled=True),
    )
    accepted_entries = 1.0 - rejected_indicator.astype(jnp.float32)
    emission_absent = lax.dynamic_slice_in_dim(regression_indicator, first_channel, ch_dev).astype(
        jnp.float32
    )
    celestial_image = accepted_entries * dividend_accumulator / normalizer_accumulated
    importance_factor = normalizer_accumulated * (
        emission_absent[:, None, None] * accepted_entries + 0.01
    )
    arrived = (
        lax.all_to_all(celestial_image, "chan", split_axis=1, concat_axis=0, tiled=True),
        lax.all_to_all(importance_factor, "chan", split_axis=1, concat_axis=0, tiled=True),
    )
    return clean_pair(arrived)


def solution(mesh):
    in_specs = (
        P("chan", "beam", None, None),
        P("beam", None, None),
        P("beam", None),
        P("chan", None, "beam"),
        P(),
    )
    out_specs = P(None, "chan", "beam")
    return jax.shard_map(local, mesh=mesh, in_specs=in_specs, out_specs=out_specs, check_vma=False)
```

profile of v0, /device:TPU:0, one launch (start us, length us, event | category | flops | bytes accessed | tf_op | source)
XLA Modules:
  0.0 1091.3 jit_solution(10178986232394698011)
XLA Ops:
  18.8 530.9 %while.16 = (s32[]{:T(128)}, f32[32,192,512]{2,0,1:T(8,128)}, f32[32,192,512]{2,0,1:T(8,128)}, s32[9,2]{0,1:T(2,128)S(1)}, f32[9,128,128]{2,1,0:T(8,128)}, /*ind...) while((s32[]{:T(128)}, f32[32,192,512]{2,0,1:T(8,128)}, ...), condition=%wide.region_1.2_spmd.clone, body=%wide.region_0.1_spmd.clone.sunk | while | flops 2621576 | bytes 35848680 | solution.py:110
  35.5 11.1 %dynamic_update_slice.18 = f32[32,192,512]{2,0,1:T(8,128)} dynamic-update-slice(f32[32,192,512]{2,0,1:T(8,128)} %get-tuple-element.275, f32[32,128,128]{2,0,1:T(8,128)S(1)} %copy.52, s32[]{:T(128)} %constant.72.clone.1..sunk, s32[]{:T(128)S(6)} %select_n.38, s32[]{:T(128)S(6)} %select_n.39) | dynamic-update-slice | bytes 4194308 | tf_op jit(solution)/shard_map/while/body/eval_jaxpr/dynamic_update_slice | solution.py:98
  49.4 11.1 %dynamic_update_slice.19 = f32[32,192,512]{2,0,1:T(8,128)} dynamic-update-slice(f32[32,192,512]{2,0,1:T(8,128)} %get-tuple-element.276, f32[32,128,128]{2,0,1:T(8,128)S(1)} %copy.53, s32[]{:T(128)} %constant.72.clone.1..sunk, s32[]{:T(128)S(6)} %select_n.38, s32[]{:T(128)S(6)} %select_n.39) | dynamic-update-slice | bytes 4194308 | tf_op jit(solution)/shard_map/while/body/eval_jaxpr/dynamic_update_slice | solution.py:103
  77.1 24.3 %dynamic_update_slice.18 = f32[32,192,512]{2,0,1:T(8,128)} dynamic-update-slice(f32[32,192,512]{2,0,1:T(8,128)} %get-tuple-element.275, f32[32,128,128]{2,0,1:T(8,128)S(1)} %copy.52, s32[]{:T(128)} %constant.72.clone.1..sunk, s32[]{:T(128)S(6)} %select_n.38, s32[]{:T(128)S(6)} %select_n.39) | dynamic-update-slice | bytes 4194308 | tf_op jit(solution)/shard_map/while/body/eval_jaxpr/dynamic_update_slice | solution.py:98
  104.2 24.3 %dynamic_update_slice.19 = f32[32,192,512]{2,0,1:T(8,128)} dynamic-update-slice(f32[32,192,512]{2,0,1:T(8,128)} %get-tuple-element.276, f32[32,128,128]{2,0,1:T(8,128)S(1)} %copy.53, s32[]{:T(128)} %constant.72.clone.1..sunk, s32[]{:T(128)S(6)} %select_n.38, s32[]{:T(128)S(6)} %select_n.39) | dynamic-update-slice | bytes 4194308 | tf_op jit(solution)/shard_map/while/body/eval_jaxpr/dynamic_update_slice | solution.py:103
  145.3 24.3 %dynamic_update_slice.18 = f32[32,192,512]{2,0,1:T(8,128)} dynamic-update-slice(f32[32,192,512]{2,0,1:T(8,128)} %get-tuple-element.275, f32[32,128,128]{2,0,1:T(8,128)S(1)} %copy.52, s32[]{:T(128)} %constant.72.clone.1..sunk, s32[]{:T(128)S(6)} %select_n.38, s32[]{:T(128)S(6)} %select_n.39) | dynamic-update-slice | bytes 4194308 | tf_op jit(solution)/shard_map/while/body/eval_jaxpr/dynamic_update_slice | solution.py:98
  172.3 24.3 %dynamic_update_slice.19 = f32[32,192,512]{2,0,1:T(8,128)} dynamic-update-slice(f32[32,192,512]{2,0,1:T(8,128)} %get-tuple-element.276, f32[32,128,128]{2,0,1:T(8,128)S(1)} %copy.53, s32[]{:T(128)} %constant.72.clone.1..sunk, s32[]{:T(128)S(6)} %select_n.38, s32[]{:T(128)S(6)} %select_n.39) | dynamic-update-slice | bytes 4194308 | tf_op jit(solution)/shard_map/while/body/eval_jaxpr/dynamic_update_slice | solution.py:103
  213.4 24.3 %dynamic_update_slice.18 = f32[32,192,512]{2,0,1:T(8,128)} dynamic-update-slice(f32[32,192,512]{2,0,1:T(8,128)} %get-tuple-element.275, f32[32,128,128]{2,0,1:T(8,128)S(1)} %copy.52, s32[]{:T(128)} %constant.72.clone.1..sunk, s32[]{:T(128)S(6)} %select_n.38, s32[]{:T(128)S(6)} %select_n.39) | dynamic-update-slice | bytes 4194308 | tf_op jit(solution)/shard_map/while/body/eval_jaxpr/dynamic_update_slice | solution.py:98
  240.5 24.3 %dynamic_update_slice.19 = f32[32,192,512]{2,0,1:T(8,128)} dynamic-update-slice(f32[32,192,512]{2,0,1:T(8,128)} %get-tuple-element.276, f32[32,128,128]{2,0,1:T(8,128)S(1)} %copy.53, s32[]{:T(128)} %constant.72.clone.1..sunk, s32[]{:T(128)S(6)} %select_n.38, s32[]{:T(128)S(6)} %select_n.39) | dynamic-update-slice | bytes 4194308 | tf_op jit(solution)/shard_map/while/body/eval_jaxpr/dynamic_update_slice | solution.py:103
  281.4 24.3 %dynamic_update_slice.18 = f32[32,192,512]{2,0,1:T(8,128)} dynamic-update-slice(f32[32,192,512]{2,0,1:T(8,128)} %get-tuple-element.275, f32[32,128,128]{2,0,1:T(8,128)S(1)} %copy.52, s32[]{:T(128)} %constant.72.clone.1..sunk, s32[]{:T(128)S(6)} %select_n.38, s32[]{:T(128)S(6)} %select_n.39) | dynamic-update-slice | bytes 4194308 | tf_op jit(solution)/shard_map/while/body/eval_jaxpr/dynamic_update_slice | solution.py:98
  308.5 24.3 %dynamic_update_slice.19 = f32[32,192,512]{2,0,1:T(8,128)} dynamic-update-slice(f32[32,192,512]{2,0,1:T(8,128)} %get-tuple-element.276, f32[32,128,128]{2,0,1:T(8,128)S(1)} %copy.53, s32[]{:T(128)} %constant.72.clone.1..sunk, s32[]{:T(128)S(6)} %select_n.38, s32[]{:T(128)S(6)} %select_n.39) | dynamic-update-slice | bytes 4194308 | tf_op jit(solution)/shard_map/while/body/eval_jaxpr/dynamic_update_slice | solution.py:103
  348.2 10.4 dynamic_update_slice.18
  361.4 10.3 dynamic_update_slice.19
  388.4 11.2 %dynamic_update_slice.18 = f32[32,192,512]{2,0,1:T(8,128)} dynamic-update-slice(f32[32,192,512]{2,0,1:T(8,128)} %get-tuple-element.275, f32[32,128,128]{2,0,1:T(8,128)S(1)} %copy.52, s32[]{:T(128)} %constant.72.clone.1..sunk, s32[]{:T(128)S(6)} %select_n.38, s32[]{:T(128)S(6)} %select_n.39) | dynamic-update-slice | bytes 4194308 | tf_op jit(solution)/shard_map/while/body/eval_jaxpr/dynamic_update_slice | solution.py:98
  402.4 11.1 %dynamic_update_slice.19 = f32[32,192,512]{2,0,1:T(8,128)} dynamic-update-slice(f32[32,192,512]{2,0,1:T(8,128)} %get-tuple-element.276, f32[32,128,128]{2,0,1:T(8,128)S(1)} %copy.53, s32[]{:T(128)} %constant.72.clone.1..sunk, s32[]{:T(128)S(6)} %select_n.38, s32[]{:T(128)S(6)} %select_n.39) | dynamic-update-slice | bytes 4194308 | tf_op jit(solution)/shard_map/while/body/eval_jaxpr/dynamic_update_slice | solution.py:103
  430.2 24.3 %dynamic_update_slice.18 = f32[32,192,512]{2,0,1:T(8,128)} dynamic-update-slice(f32[32,192,512]{2,0,1:T(8,128)} %get-tuple-element.275, f32[32,128,128]{2,0,1:T(8,128)S(1)} %copy.52, s32[]{:T(128)} %constant.72.clone.1..sunk, s32[]{:T(128)S(6)} %select_n.38, s32[]{:T(128)S(6)} %select_n.39) | dynamic-update-slice | bytes 4194308 | tf_op jit(solution)/shard_map/while/body/eval_jaxpr/dynamic_update_slice | solution.py:98
  457.3 24.3 %dynamic_update_slice.19 = f32[32,192,512]{2,0,1:T(8,128)} dynamic-update-slice(f32[32,192,512]{2,0,1:T(8,128)} %get-tuple-element.276, f32[32,128,128]{2,0,1:T(8,128)S(1)} %copy.53, s32[]{:T(128)} %constant.72.clone.1..sunk, s32[]{:T(128)S(6)} %select_n.38, s32[]{:T(128)S(6)} %select_n.39) | dynamic-update-slice | bytes 4194308 | tf_op jit(solution)/shard_map/while/body/eval_jaxpr/dynamic_update_slice | solution.py:103
  498.4 24.3 %dynamic_update_slice.18 = f32[32,192,512]{2,0,1:T(8,128)} dynamic-update-slice(f32[32,192,512]{2,0,1:T(8,128)} %get-tuple-element.275, f32[32,128,128]{2,0,1:T(8,128)S(1)} %copy.52, s32[]{:T(128)} %constant.72.clone.1..sunk, s32[]{:T(128)S(6)} %select_n.38, s32[]{:T(128)S(6)} %select_n.39) | dynamic-update-slice | bytes 4194308 | tf_op jit(solution)/shard_map/while/body/eval_jaxpr/dynamic_update_slice | solution.py:98
  525.4 24.3 %dynamic_update_slice.19 = f32[32,192,512]{2,0,1:T(8,128)} dynamic-update-slice(f32[32,192,512]{2,0,1:T(8,128)} %get-tuple-element.276, f32[32,128,128]{2,0,1:T(8,128)S(1)} %copy.53, s32[]{:T(128)} %constant.72.clone.1..sunk, s32[]{:T(128)S(6)} %select_n.38, s32[]{:T(128)S(6)} %select_n.39) | dynamic-update-slice | bytes 4194308 | tf_op jit(solution)/shard_map/while/body/eval_jaxpr/dynamic_update_slice | solution.py:103
  550.6 213.1 %reduce-scatter.5.cloned.1.call-done = f32[32,192,128]{2,0,1:T(8,128)} async-done(((f32[32,192,512]{2,0,1:T(8,128)}), f32[32,192,128]{2,0,1:T(8,128)}) %reduce-scatter.5.cloned.1.call-update) | async-done | bytes 3145744 | tf_op jit(solution)/shard_map/reduce_scatter | solution.py:113
  763.7 215.3 %reduce-scatter.3.cloned.1.call-done = f32[32,192,128]{2,0,1:T(8,128)} async-done(((f32[32,192,512]{2,0,1:T(8,128)}), f32[32,192,128]{2,0,1:T(8,128)}) %reduce-scatter.3.cloned.1.call-update) | async-done | bytes 3145744 | tf_op jit(solution)/shard_map/reduce_scatter | solution.py:112
  979.0 6.8 add_multiply_fusion
  985.8 41.4 %all_to_all.30 = f32[32,192,128]{2,0,1:T(8,128)} all-to-all(f32[32,192,128]{2,0,1:T(8,128)S(1)} %get-tuple-element.197), channel_id=1, replica_groups=mesh['chan'=8,'beam'=4] {'chan'}, dimensions={1} | all-to-all | bytes 6291456 | tf_op jit(solution)/shard_map/all_to_all | solution.py:124
  1035.7 33.9 %all-to-all-done.1 = f32[32,192,128]{2,0,1:T(8,128)} async-done(((f32[32,192,128]{2,0,1:T(8,128)}), f32[32,192,128]{2,0,1:T(8,128)}, u32[]{:S(2)}, u32[]{:S(2)}) %all-to-all-start.1) | async-done | bytes 3145760 | tf_op jit(solution)/shard_map/all_to_all | solution.py:125
  (97 shorter events, 176.6 us)
Async XLA Ops:
  6.5 757.2 %reduce-scatter.5.cloned.1.call-start = ((), (), s32[]{:S(2)}) async-start(), calls=%async_computation.5 | async-start | bytes 15728640 | tf_op jit(solution)/shard_map/reduce_scatter | solution.py:113
  12.7 6.1 copy-start.1
  549.8 429.2 %reduce-scatter.3.cloned.1.call-start = ((), (), s32[]{:S(2)}) async-start(), calls=%async_computation.4 | async-start | bytes 15728640 | tf_op jit(solution)/shard_map/reduce_scatter | solution.py:112
  549.8 0.7 copy-start.2
  549.8 429.2 %copy-start = (s32[32,192,128]{2,1,0:T(8,128)S(1)}, s32[32,192,128]{2,1,0:T(8,128)}, u32[]{:S(2)}) copy-start(s32[32,192,128]{2,1,0:T(8,128)} %param.10) | copy-start | bytes 9437188
  1027.2 42.4 %all-to-all-start.1 = ((f32[32,192,128]{2,0,1:T(8,128)}), f32[32,192,128]{2,0,1:T(8,128)}, u32[]{:S(2)}, u32[]{:S(2)}) async-start(f32[32,192,128]{2,0,1:T(8,128)} %get-tuple-element.196), calls=%async_computation.3 | async-start | bytes 6291456 | tf_op jit(solution)/shard_map/all_to_all | solution.py:125
Sparse Core Ops, SparseCore 0:
  549.9 213.7 reduce-scatter.4
  766.1 212.8 reduce-scatter.2
where the time goes:
time: 1090 us
  local copies, waits for them, and re-layouts  469 us (43%)
  waiting for transfers between devices  463 us (42%)
  other arithmetic  58.2 us (5%)
  blocking collectives  41.4 us (4%)
  loops' own time  34.4 us (3%)
  between operations  13.5 us (1%)
    reduce_scatter x1, waiting for transfers between devices, local(): lax.psum_scatter(dividend_accumulator, 'beam', scatter_dimension=2, tiled...  215 us
    reduce_scatter x1, waiting for transfers between devices, local(): lax.psum_scatter(normalizer_accumulated, 'beam', scatter_dimension=2, til...  213 us
    dynamic_update_slice x18, local copies, waits for them, and re-layouts, place(): lax.dynamic_update_slice(normalizer_accumulated, lax.dynamic_slice(normal...  203 us
    dynamic_update_slice x18, local copies, waits for them, and re-layouts, place(): lax.dynamic_update_slice(dividend_accumulator, lax.dynamic_slice(dividend...  189 us
    add x9, other arithmetic, place(): lax.dynamic_slice(normalizer_accumulated, corner, extent)  49.6 us
    all_to_all x1, blocking collectives, local(): lax.all_to_all(celestial_image, 'chan', split_axis=1, concat_axis=0, tile...  41.4 us
    dynamic_slice x9, local copies, waits for them, and re-layouts, place(): lax.dynamic_slice(normalizer_accumulated, corner, extent)  40.8 us
    another operation x1, loops' own time, local(): lax.fori_loop(0, beam_dev, place, (empty, empty))  34.4 us
  transfers between devices with their start and end apart: 3, of which 3 were waited for; matrix products, arithmetic and copies ran while one was open for 0% of the time, Pallas kernels for 0%

commit v1 on v0

v1 whole, which is shorter than its diff:
```python
import functools

import jax
import jax.numpy as jnp
from jax import lax
from jax.experimental import pallas as pl
from jax.experimental.pallas import tpu as pltpu
from jax.sharding import PartitionSpec as P

MOS_ROWS = 192
MOS_COLS = 512
GRID = 6
JITTER = 16
LANES = 128
OUTSIDE = -1.0e4
MESH = pl.DeviceIdType.MESH


def start_range(position, span):
    if position == 0:
        return 0, 0
    if position == GRID - 1:
        return span, span
    middle = position * span // (GRID - 1)
    return max(0, middle - JITTER), min(span, middle + JITTER)


def covered_rows(group, beams_each, side, block):
    first, last = MOS_ROWS, 0
    for beam in range(group * beams_each, (group + 1) * beams_each):
        low, high = start_range(beam % GRID, MOS_COLS - side)
        if high + side <= block * LANES or low >= (block + 1) * LANES:
            continue
        low, high = start_range(beam // GRID, MOS_ROWS - side)
        first, last = min(first, low), max(last, high + side)
    return first // 8 * 8, min(MOS_ROWS, -(-last // 8) * 8)


def place_kernel(
    where_ref, offsets_ref, image_ref, weight_ref, sums_ref, tiles_ref, log_ref, plane_ref, *, slope
):
    step = pl.program_id(0)
    blocks, depth, _, _ = sums_ref.shape
    beams, side, _ = weight_ref.shape
    tile_rows = tiles_ref.shape[2]
    piece = 32
    lane = lax.broadcasted_iota(jnp.int32, (piece, LANES), 1)

    def corner(beam):
        row, col = offsets_ref[beam, 0], offsets_ref[beam, 1]
        return row, lax.shift_right_logical(col, 7), jnp.bitwise_and(col, LANES - 1)

    @pl.when(step == 0)
    def _():
        log_ref[...] = jnp.log(weight_ref[...])

        def spread(beam, carry):
            row, block, shift = corner(beam)
            plane_ref[...] = jnp.full(plane_ref.shape, OUTSIDE, jnp.float32)

            def part(index, inner):
                start = pl.multiple_of(index * piece, piece)
                value = pltpu.roll(log_ref[beam, pl.ds(start, piece), :], shift, 1)
                plane_ref[block, pl.ds(row + start, piece), :] = jnp.where(
                    lane >= shift, value, OUTSIDE
                )

                @pl.when(block < blocks - 1)
                def _():
                    plane_ref[block + 1, pl.ds(row + start, piece), :] = jnp.where(
                        lane < shift, value, OUTSIDE
                    )

                return inner

            lax.fori_loop(0, side // piece, part, 0)
            tiles_ref[:, beam, :, :] = plane_ref[:, pl.ds(where_ref[1], tile_rows), :]
            return carry

        lax.fori_loop(0, beams, spread, 0)

    sums_ref[...] = jnp.zeros(sums_ref.shape, jnp.float32)
    exponent = 1.0 + slope * (where_ref[0] + step * depth).astype(jnp.float32)

    def add_beam(beam, carry):
        row, block, shift = corner(beam)
        after = jnp.minimum(block + 1, blocks - 1)

        def part(index, inner):
            start = pl.multiple_of(index * piece, piece)
            rows = pl.ds(row + start, piece)
            logs = log_ref[beam, pl.ds(start, piece), :]
            response = jnp.exp(exponent * logs)
            ratio = jnp.exp(slope * logs)
            for channel in range(depth):
                value = image_ref[channel, beam, pl.ds(start, piece), :] * response
                value = pltpu.roll(value, shift, 1)
                sums_ref[block, channel, rows, :] += jnp.where(lane >= shift, value, 0.0)
                sums_ref[after, channel, rows, :] += jnp.where(lane < shift, value, 0.0)
                response = response * ratio
            return inner

        lax.fori_loop(0, side // piece, part, 0)
        return carry

    lax.fori_loop(0, beams, add_beam, 0)


def place(where, offsets, images, beam_weight, blocks, tile_rows, channels):
    ch_dev, beams, side, _ = images.shape
    depth = 4
    return pl.pallas_call(
        functools.partial(place_kernel, slope=0.5 / (channels - 1)),
        grid=(ch_dev // depth,),
        in_specs=[
            pl.BlockSpec(memory_space=pltpu.SMEM),
            pl.BlockSpec(memory_space=pltpu.SMEM),
            pl.BlockSpec((depth, beams, side, side), lambda s: (s, 0, 0, 0)),
            pl.BlockSpec((beams, side, side), lambda s: (0, 0, 0)),
        ],
        out_specs=[
            pl.BlockSpec((blocks, depth, MOS_ROWS, LANES), lambda s: (0, s, 0, 0)),
            pl.BlockSpec((blocks, beams, tile_rows, LANES), lambda s: (0, 0, 0, 0)),
        ],
        out_shape=[
            jax.ShapeDtypeStruct((blocks, ch_dev, MOS_ROWS, LANES), jnp.float32),
            jax.ShapeDtypeStruct((blocks, beams, tile_rows, LANES), jnp.float32),
        ],
        scratch_shapes=[
            pltpu.VMEM((beams, side, side), jnp.float32),
            pltpu.VMEM((blocks, MOS_ROWS, LANES), jnp.float32),
        ],
        compiler_params=pltpu.CompilerParams(vmem_limit_bytes=48 << 20),
        name="place_beams",
    )(where, offsets, images, beam_weight)


def exchange_kernel(
    sums_ref,
    flags_ref,
    logs_ref,
    sky_out,
    flag_out,
    log_out,
    own,
    up,
    down,
    rowed,
    own_sem,
    keep_sem,
    up_recv,
    down_recv,
    up_send,
    down_send,
    sky_send,
    sky_recv,
    flag_send,
    flag_recv,
    log_send,
    log_recv,
    *,
    groups,
    tiles,
    depth,
    reach_up,
    reach_down,
):
    group = lax.axis_index("beam")
    tile = lax.axis_index("chan")
    ch_dev = sums_ref.shape[1]
    tile_rows = flags_ref.shape[2]
    beams = logs_ref.shape[1]
    steps = ch_dev // depth

    others = [lax.rem(tile + k, tiles) for k in range(1, tiles)]
    columns = [lax.rem(group + k, groups) for k in range(1, groups)]

    barrier = pltpu.get_barrier_semaphore()
    for other in others:
        pl.semaphore_signal(barrier, inc=1, device_id={"chan": other}, device_id_type=MESH)
    for other in columns:
        pl.semaphore_signal(barrier, inc=1, device_id={"beam": other}, device_id_type=MESH)

    def load(step):
        span = pl.ds(step * depth, depth)
        return pltpu.make_async_copy(sums_ref.at[:, span], own.at[:, span], own_sem.at[step])

    def fetch(step, carry):
        load(step).start()
        return carry

    lax.fori_loop(0, steps, fetch, 0)
    mine = pl.ds(tile * ch_dev, ch_dev)
    kept = [
        pltpu.make_async_copy(flags_ref.at[:, tile], flag_out.at[mine], keep_sem.at[0]),
        pltpu.make_async_copy(
            logs_ref.at[group], log_out.at[pl.ds(group * beams, beams)], keep_sem.at[1]
        ),
    ]
    for copy in kept:
        copy.start()
    pl.semaphore_wait(barrier, len(others) + len(columns))

    small = []
    for k, other in enumerate(columns):
        small.append(
            pltpu.make_async_remote_copy(
                src_ref=logs_ref.at[other],
                dst_ref=log_out.at[pl.ds(group * beams, beams)],
                send_sem=log_send.at[k],
                recv_sem=log_recv.at[k],
                device_id={"beam": other},
                device_id_type=MESH,
            )
        )
    for k, other in enumerate(others):
        small.append(
            pltpu.make_async_remote_copy(
                src_ref=flags_ref.at[:, other],
                dst_ref=flag_out.at[mine],
                send_sem=flag_send.at[k],
                recv_sem=flag_recv.at[k],
                device_id={"chan": other},
                device_id_type=MESH,
            )
        )
    for copy in small:
        copy.start()

    def up_copy(z, block, step):
        span, rows = pl.ds(step * depth, depth), pl.ds(0, reach_up[z, block])
        source = own.at[block, span, rows] if z == 0 else up.at[block - 1, span, rows]
        return pltpu.make_async_remote_copy(
            src_ref=source,
            dst_ref=up.at[block - 1, span, rows],
            send_sem=up_send.at[block],
            recv_sem=up_recv.at[step, block],
            device_id={"beam": z + 1},
            device_id_type=MESH,
        )

    def down_copy(z, block, step):
        first = reach_down[z, block]
        span, rows = pl.ds(step * depth, depth), pl.ds(first, MOS_ROWS - first)
        source = own.at[block, span, rows] if z == groups - 1 else down.at[block, span, rows]
        return pltpu.make_async_remote_copy(
            src_ref=source,
            dst_ref=down.at[block, span, rows],
            send_sem=down_send.at[block],
            recv_sem=down_recv.at[step, block],
            device_id={"beam": z - 1},
            device_id_type=MESH,
        )

    def sky_copy(k, other, span):
        return pltpu.make_async_remote_copy(
            src_ref=rowed.at[other, span],
            dst_ref=sky_out.at[pl.ds(tile * ch_dev + span.start, span.size)],
            send_sem=sky_send.at[k],
            recv_sem=sky_recv.at[k],
            device_id={"chan": other},
            device_id_type=MESH,
        )

    for z in range(groups):

        @pl.when(group == z)
        def _(z=z):
            def work(step, carry):
                span = pl.ds(step * depth, depth)
                load(step).wait()
                for block in range(groups - 1, z, -1):
                    if z > 0:
                        old, new = reach_up[z - 1, block], reach_up[z, block]
                        up_copy(z - 1, block, step).wait_recv()
                        up[block - 1, span, 0:old, :] += own[block, span, 0:old, :]
                        if new > old:
                            up[block - 1, span, old:new, :] = own[block, span, old:new, :]
                    up_copy(z, block, step).start()
                for block in range(z):
                    if z < groups - 1:
                        old, new = reach_down[z + 1, block], reach_down[z, block]
                        down_copy(z + 1, block, step).wait_recv()
                        down[block, span, old:, :] += own[block, span, old:, :]
                        if new < old:
                            down[block, span, new:old, :] = own[block, span, new:old, :]
                    down_copy(z, block, step).start()
                if z > 0:
                    old = reach_up[z - 1, z]
                    up_copy(z - 1, z, step).wait_recv()
                    own[z, span, 0:old, :] += up[z - 1, span, 0:old, :]
                if z < groups - 1:
                    old = reach_down[z + 1, z]
                    down_copy(z + 1, z, step).wait_recv()
                    own[z, span, old:, :] += down[z, span, old:, :]
                for index in range(tiles):
                    rowed[index, span, :, :] = own[
                        z, span, index * tile_rows : (index + 1) * tile_rows, :
                    ]
                for k, other in enumerate(others):
                    sky_copy(k, other, span).start()
                return carry

            lax.fori_loop(0, steps, work, 0)
            for block in range(z + 1, groups):
                ref = up.at[block - 1, :, pl.ds(0, reach_up[z, block])]
                pltpu.make_async_copy(ref, ref, up_send.at[block]).wait()
            for block in range(z):
                first = reach_down[z, block]
                ref = down.at[block, :, pl.ds(first, MOS_ROWS - first)]
                pltpu.make_async_copy(ref, ref, down_send.at[block]).wait()

    kept.append(pltpu.make_async_copy(rowed.at[tile], sky_out.at[mine], keep_sem.at[2]))
    kept[-1].start()
    for copy in small:
        copy.wait()
    for k, other in enumerate(others):
        sky_copy(k, other, pl.ds(0, ch_dev)).wait()
    for copy in kept:
        copy.wait()


def exchange(sums, flags, logs, groups, tiles):
    ch_dev = sums.shape[1]
    tile_rows = flags.shape[2]
    beams = logs.shape[1]
    depth = 2
    steps = ch_dev // depth
    side = MOS_ROWS - start_range(GRID - 1, MOS_ROWS - LANES)[0]
    reach_up, reach_down = {}, {}
    for block in range(groups):
        rows = [covered_rows(group, beams, side, block) for group in range(groups)]
        for z in range(groups):
            reach_up[z, block] = max(high for _, high in rows[: z + 1])
            reach_down[z, block] = min(low for low, _ in rows[z:])
    dma = pltpu.SemaphoreType.DMA
    any_space = pl.BlockSpec(memory_space=pl.ANY)
    return pl.pallas_call(
        functools.partial(
            exchange_kernel,
            groups=groups,
            tiles=tiles,
            depth=depth,
            reach_up=reach_up,
            reach_down=reach_down,
        ),
        in_specs=[any_space] * 3,
        out_specs=[any_space] * 3,
        out_shape=[
            jax.ShapeDtypeStruct((tiles * ch_dev, tile_rows, LANES), jnp.float32),
            jax.ShapeDtypeStruct((tiles * ch_dev, tile_rows, LANES), jnp.int32),
            jax.ShapeDtypeStruct((groups * beams, tile_rows, LANES), jnp.float32),
        ],
        scratch_shapes=[
            pltpu.VMEM((groups, ch_dev, MOS_ROWS, LANES), jnp.float32),
            pltpu.VMEM((groups - 1, ch_dev, MOS_ROWS, LANES), jnp.float32),
            pltpu.VMEM((groups - 1, ch_dev, MOS_ROWS, LANES), jnp.float32),
            pltpu.VMEM((tiles, ch_dev, tile_rows, LANES), jnp.float32),
            dma((steps,)),
            dma((3,)),
            dma((steps, groups)),
            dma((steps, groups)),
            dma((groups,)),
            dma((groups,)),
            dma((tiles - 1,)),
            dma((tiles - 1,)),
            dma((tiles - 1,)),
            dma((tiles - 1,)),
            dma((groups - 1,)),
            dma((groups - 1,)),
        ],
        compiler_params=pltpu.CompilerParams(
            collective_id=0, has_side_effects=True, vmem_limit_bytes=56 << 20
        ),
        name="exchange",
    )(sums, flags, logs)


def solve_cubic(normal_matrix, right_side):
    factor = {}
    for outer in range(4):
        for inner in range(outer + 1):
            value = normal_matrix[outer, inner]
            for other in range(inner):
                value = value - factor[outer, other] * factor[inner, other]
            if outer == inner:
                factor[outer, outer] = jnp.sqrt(value)
            else:
                factor[outer, inner] = value / factor[inner, inner]
    forward = []
    for outer in range(4):
        value = right_side[outer]
        for other in range(outer):
            value = value - factor[outer, other] * forward[other]
        forward.append(value / factor[outer, outer])
    backward = [None] * 4
    for outer in range(3, -1, -1):
        value = forward[outer]
        for other in range(outer + 1, 4):
            value = value - factor[other, outer] * backward[other]
        backward[outer] = value / factor[outer, outer]
    return backward


POLYNOMIALS = (
    {0: 1.0},
    {1: 1.0},
    {0: -0.5, 2: 1.5},
    {1: -1.5, 3: 2.5},
)


def fit_kernel(where_ref, regression_ref, sky_ref, flag_ref, log_ref, out_ref, total_ref, *, slope):
    channels, rows, _ = sky_ref.shape
    piece = 8 if rows % 8 == 0 else rows
    run = 16
    first = where_ref[0]
    beams = [(r * GRID, q) for r in range(GRID) for q in range(3)]

    def totals(index, carry):
        start = index * run
        exponent = 1.0 + slope * start.astype(jnp.float32)
        for part in range(rows // piece):
            span = pl.ds(part * piece, piece)
            total = [jnp.zeros((piece, LANES), jnp.float32)] * run
            for begin, q in beams:
                logs = log_ref[begin + q + first, span, :]
                value = jnp.exp((2.0 * exponent) * logs)
                ratio = jnp.exp((2.0 * slope) * logs)
                for k in range(run):
                    total[k] = total[k] + value
                    if k < run - 1:
                        value = value * ratio
            for k in range(run):
                total_ref[start + k, span, :] = total[k]
        return carry

    lax.fori_loop(0, channels // run, totals, 0)

    def position(channel):
        return (2.0 * channel.astype(jnp.float32) + 1.0) * (1.0 / channels) - 1.0

    def gather(channel, carry):
        powers, rights = list(carry[:7]), list(carry[7:])
        x = position(channel)
        open_sky = 1.0 - flag_ref[channel].astype(jnp.float32)
        total = total_ref[channel]
        sky = open_sky * sky_ref[channel] / total
        total_ref[channel] = sky
        chosen = regression_ref[channel].astype(jnp.float32)
        weight = total * (chosen * open_sky + 0.01)
        right = weight * sky
        for k in range(7):
            powers[k] = powers[k] + weight
            if k < 6:
                weight = weight * x
        for k in range(4):
            rights[k] = rights[k] + right
            if k < 3:
                right = right * x
        return tuple(powers) + tuple(rights)

    zero = jnp.zeros((rows, LANES), jnp.float32)
    sums = lax.fori_loop(0, channels, gather, (zero,) * 11, unroll=4)
    powers, rights = sums[:7], sums[7:]
    normal = {}
    for outer in range(4):
        for inner in range(outer + 1):
            terms = {}
            for a, u in POLYNOMIALS[outer].items():
                for b, v in POLYNOMIALS[inner].items():
                    terms[a + b] = terms.get(a + b, 0.0) + u * v
            normal[outer, inner] = sum(v * powers[k] for k, v in terms.items())
    right_side = [sum(v * rights[k] for k, v in POLYNOMIALS[o].items()) for o in range(4)]
    fitted = solve_cubic(normal, right_side)

    def residual(channel):
        x = position(channel)
        square = x * x
        continuum = (
            fitted[0]
            + x * fitted[1]
            + (0.5 * (3.0 * square - 1.0)) * fitted[2]
            + (0.5 * (5.0 * square * x - 3.0 * x)) * fitted[3]
        )
        return total_ref[channel] - continuum

    def smooth(channel, carry):
        before, here = carry
        after = residual(channel + 1)
        out_ref[channel] = 0.25 * before + 0.5 * here + 0.25 * after
        return here, after

    before, here = lax.fori_loop(
        0, channels - 1, smooth, (zero, residual(jnp.int32(0))), unroll=3
    )
    out_ref[channels - 1] = 0.25 * before + 0.5 * here


def fit(where, regression, sky, flags, logs):
    channels = sky.shape[0]
    smem = pl.BlockSpec(memory_space=pltpu.SMEM)
    vmem = pl.BlockSpec(memory_space=pltpu.VMEM)
    return pl.pallas_call(
        functools.partial(fit_kernel, slope=0.5 / (channels - 1)),
        in_specs=[smem, smem, vmem, vmem, vmem],
        out_specs=vmem,
        out_shape=jax.ShapeDtypeStruct(sky.shape, jnp.float32),
        scratch_shapes=[pltpu.VMEM(sky.shape, jnp.float32)],
        compiler_params=pltpu.CompilerParams(vmem_limit_bytes=48 << 20),
        name="fit",
    )(where, regression, sky, flags, logs)


def local(
    images, beam_weight, offsets, rejected_indicator, regression_indicator, *, groups, tiles
):
    ch_dev = images.shape[0]
    channels = regression_indicator.shape[0]
    tile_rows = MOS_ROWS // tiles
    tile = lax.axis_index("chan")
    group = lax.axis_index("beam")
    where = jnp.stack([tile * ch_dev, tile * tile_rows]).astype(jnp.int32)
    sums, logs = place(where, offsets, images, beam_weight, groups, tile_rows, channels)
    flags = rejected_indicator.reshape(ch_dev, tiles, tile_rows, rejected_indicator.shape[2])
    sky, flags, logs = exchange(sums, flags, logs, groups, tiles)
    return fit(group[None].astype(jnp.int32), regression_indicator, sky, flags, logs)


def solution(mesh):
    in_specs = (
        P("chan", "beam", None, None),
        P("beam", None, None),
        P("beam", None),
        P("chan", None, "beam"),
        P(),
    )
    out_specs = P(None, "chan", "beam")
    body = functools.partial(local, groups=mesh.shape["beam"], tiles=mesh.shape["chan"])
    return jax.shard_map(body, mesh=mesh, in_specs=in_specs, out_specs=out_specs, check_vma=False)
```

time: 1090 us -> 363 us (0.33)
  local copies, waits for them, and re-layouts: 469 us -> 5.49 us
  waiting for transfers between devices: 463 us -> 0 us
  Pallas kernels: 0 us -> 357 us
  other arithmetic: 58.2 us -> 0.07 us
  blocking collectives: 41.4 us -> 0 us
  loops' own time: 34.4 us -> 0 us
  between operations: 13.5 us -> 0.03 us
    reduce_scatter x2 -> x0, waiting for transfers between devices: 428 us -> none  [the longest x1 215 us: local(): lax.psum_scatter(dividend_accumulator, 'beam', scatter_dimension=2, tiled...]
    dynamic_update_slice x36 -> x0, local copies, waits for them, and re-layouts: 393 us -> none  [the longest x18 203 us: place(): lax.dynamic_update_slice(normalizer_accumulated, lax.dynamic_slice(normal...]
    pallas_call x0 -> x3, Pallas kernels: none -> 357 us  [the longest x1 304 us: exchange(): pl.pallas_call(functools.partial(exchange_kernel, groups=groups, tiles=ti...]
    add x18 -> x0, other arithmetic: 49.7 us -> none  [the longest x9 49.6 us: place(): lax.dynamic_slice(normalizer_accumulated, corner, extent)]
    dynamic_slice x18 -> x0, local copies, waits for them, and re-layouts: 46.6 us -> none  [the longest x9 40.8 us: place(): lax.dynamic_slice(normalizer_accumulated, corner, extent)]
    all_to_all x1 -> x0, blocking collectives: 41.4 us -> none  [local(): lax.all_to_all(celestial_image, 'chan', split_axis=1, concat_axis=0, tile...]
    another operation x1 -> x0, loops' own time: 34.4 us -> none  [local(): lax.fori_loop(0, beam_dev, place, (empty, empty))]
    all_to_all x1 -> x0, waiting for transfers between devices: 33.9 us -> none  [local(): lax.all_to_all(importance_factor, 'chan', split_axis=1, concat_axis=0, ti...]
  transfers between devices with their start and end apart: 3 -> 0, of which waited for: 3 -> 0; matrix products, arithmetic and copies ran while one was open for 0% -> 0% of each run, Pallas kernels for 0% -> 0%
where the time goes in v1:
time: 363 us
  Pallas kernels  357 us (98%)
  local copies, waits for them, and re-layouts  5.49 us (2%)
    pallas_call x1, Pallas kernels, exchange(): pl.pallas_call(functools.partial(exchange_kernel, groups=groups, tiles=ti...  304 us
    pallas_call x1, Pallas kernels, place(): pl.pallas_call(functools.partial(place_kernel, slope=0.5 / (channels - 1)...  38.9 us
    pallas_call x1, Pallas kernels, fit(): pl.pallas_call(functools.partial(fit_kernel, slope=0.5 / (channels - 1)),...  14.2 us

profile of v1, /device:TPU:0, one launch (start us, length us, event | category | flops | bytes accessed | tf_op | source)
XLA Modules:
  0.0 362.8 jit_solution(7717053096704225035)
XLA Ops:
  0.0 0.1 pad_add_fusion.where_ref
  0.1 0.8 copy.6.offsets_ref
  0.8 0.0 copy-start.1
  0.8 1.1 copy-done.1
  1.9 38.9 %place_beams.1 = (f32[4,32,192,128]{3,2,1,0:T(8,128)}, f32[4,9,24,128]{3,2,1,0:T(8,128)S(1)}) custom-call(s32[2]{0:T(128)S(1)} %pad_add_fusion.where_ref, s32[9,2]{1,0:T(8,128)S(1)} %copy.6.offsets_ref, f32[32,9,128,128]{3,2,1,0:T(8,128)} %image_ref.1, f32[9,128,128]{2,1,0:T(8,128)S(1)} %copy-done.1), custom_call_target="tpu_custom_call" | custom-call | tf_op jit(solution)/shard_map/place_beams/pallas_call | solution.py:112
  40.8 0.0 copy-start.2
  40.8 0.8 copy-done.2
  41.6 0.0 copy-start.4
  41.6 304.1 %exchange.1 = (f32[256,24,128]{2,1,0:T(8,128)}, s32[256,24,128]{2,1,0:T(8,128)}, f32[36,24,128]{2,1,0:T(8,128)}) custom-call(f32[4,32,192,128]{3,2,1,0:T(8,128)} %get-tuple-element.10.sums_ref, s32[32,8,24,128]{3,2,1,0:T(8,128)} %bitcast.4, f32[4,9,24,128]{3,2,1,0:T(8,128)} %copy-done.2), custom_call_target="tpu_custom_call" | custom-call | tf_op jit(solution)/shard_map/exchange/pallas_call | solution.py:338
  345.7 0.0 copy-done.4
  345.7 0.0 copy-start
  345.7 1.9 copy-done
  347.6 0.0 copy-start.3
  347.6 1.0 copy-done.3
  348.6 14.2 %fit.1 = f32[256,24,128]{2,1,0:T(8,128)} custom-call(s32[1]{0:T(128)} %bitcast.where_ref, s32[256]{0:T(256)S(1)} %copy-done.4, f32[256,24,128]{2,1,0:T(8,128)S(1)} %copy-done, s32[256,24,128]{2,1,0:T(8,128)} %get-tuple-element.13.flag_ref, f32[36,24,128]{2,1,0:T(8,128)S(1)} %copy-done.3), custom_call_target="tpu_custom_call" | custom-call | tf_op jit(solution)/shard_map/fit/pallas_call | solution.py:504
Async XLA Ops:
  0.8 1.1 copy-start.1
  40.8 0.8 copy-start.2
  41.6 304.1 %copy-start.4 = (s32[256]{0:T(256)S(1)}, s32[256]{0:T(256)}, u32[]{:S(2)}) copy-start(s32[256]{0:T(256)} %regression_ref.1) | copy-start | bytes 3076
  345.7 1.9 copy-start
  347.6 1.0 copy-start.3

commit v2 on v1

--- a/solution.py
+++ b/solution.py
@@ -43,7 +43,7 @@
     blocks, depth, _, _ = sums_ref.shape
     beams, side, _ = weight_ref.shape
     tile_rows = tiles_ref.shape[2]
-    piece = 32
+    piece = 64
     lane = lax.broadcasted_iota(jnp.int32, (piece, LANES), 1)
 
     def corner(beam):
@@ -92,12 +92,18 @@
             logs = log_ref[beam, pl.ds(start, piece), :]
             response = jnp.exp(exponent * logs)
             ratio = jnp.exp(slope * logs)
+            values = []
             for channel in range(depth):
                 value = image_ref[channel, beam, pl.ds(start, piece), :] * response
-                value = pltpu.roll(value, shift, 1)
-                sums_ref[block, channel, rows, :] += jnp.where(lane >= shift, value, 0.0)
-                sums_ref[after, channel, rows, :] += jnp.where(lane < shift, value, 0.0)
+                values.append(pltpu.roll(value, shift, 1))
                 response = response * ratio
+            for target, inside in ((block, lane >= shift), (after, lane < shift)):
+                sums = [
+                    sums_ref[target, channel, rows, :] + jnp.where(inside, value, 0.0)
+                    for channel, value in enumerate(values)
+                ]
+                for channel, value in enumerate(sums):
+                    sums_ref[target, channel, rows, :] = value
             return inner
 
         lax.fori_loop(0, side // piece, part, 0)
@@ -266,9 +272,12 @@
 
         @pl.when(group == z)
         def _(z=z):
-            def work(step, carry):
+            lower = 2 * z < groups
+            up_lag, down_lag = (0, 2) if lower else (2, 0)
+            last_lag = 6 if z in (0, groups - 1) else 3
+
+            def pass_up(step):
                 span = pl.ds(step * depth, depth)
-                load(step).wait()
                 for block in range(groups - 1, z, -1):
                     if z > 0:
                         old, new = reach_up[z - 1, block], reach_up[z, block]
@@ -277,6 +286,9 @@
                         if new > old:
                             up[block - 1, span, old:new, :] = own[block, span, old:new, :]
                     up_copy(z, block, step).start()
+
+            def pass_down(step):
+                span = pl.ds(step * depth, depth)
                 for block in range(z):
                     if z < groups - 1:
                         old, new = reach_down[z + 1, block], reach_down[z, block]
@@ -285,6 +297,9 @@
                         if new < old:
                             down[block, span, new:old, :] = own[block, span, new:old, :]
                     down_copy(z, block, step).start()
+
+            def finish(step):
+                span = pl.ds(step * depth, depth)
                 if z > 0:
                     old = reach_up[z - 1, z]
                     up_copy(z - 1, z, step).wait_recv()
@@ -299,9 +314,21 @@
                     ]
                 for k, other in enumerate(others):
                     sky_copy(k, other, span).start()
+
+            def work(turn, carry):
+                @pl.when(turn < steps)
+                def _():
+                    load(turn).wait()
+
+                for lag, act in ((up_lag, pass_up), (down_lag, pass_down), (last_lag, finish)):
+
+                    @pl.when(jnp.logical_and(turn >= lag, turn < steps + lag))
+                    def _(lag=lag, act=act):
+                        act(turn - lag)
+
                 return carry
 
-            lax.fori_loop(0, steps, work, 0)
+            lax.fori_loop(0, steps + last_lag, work, 0)
             for block in range(z + 1, groups):
                 ref = up.at[block - 1, :, pl.ds(0, reach_up[z, block])]
                 pltpu.make_async_copy(ref, ref, up_send.at[block]).wait()

time: 363 us -> 231 us (0.64)
  Pallas kernels: 357 us -> 225 us
    pallas_call x1, Pallas kernels: 304 us -> 187 us  [exchange(): pl.pallas_call(functools.partial(exchange_kernel, groups=groups, tiles=ti...]
    pallas_call x1, Pallas kernels: 38.9 us -> 23.8 us  [place(): pl.pallas_call(functools.partial(place_kernel, slope=0.5 / (channels - 1)...]
where the time goes in v2:
time: 231 us; the launch traced here: 230 us
  Pallas kernels  225 us (97%)
  local copies, waits for them, and re-layouts  5.49 us (2%)
    pallas_call x1, Pallas kernels, exchange(): pl.pallas_call(functools.partial(exchange_kernel, groups=groups, tiles=ti...  187 us
    pallas_call x1, Pallas kernels, place(): pl.pallas_call(functools.partial(place_kernel, slope=0.5 / (channels - 1)...  23.8 us
    pallas_call x1, Pallas kernels, fit(): pl.pallas_call(functools.partial(fit_kernel, slope=0.5 / (channels - 1)),...  14.2 us
    unnamed x11, local copies, waits for them, and re-layouts  5.49 us

profile of v2, /device:TPU:0, one launch (start us, length us, event | category | flops | bytes accessed | tf_op | source)
XLA Modules:
  0.0 230.3 jit_solution(14588705787344275897)
XLA Ops:
  0.0 0.1 pad_add_fusion.where_ref
  0.1 0.8 copy.6.offsets_ref
  0.8 0.0 copy-start.1
  0.8 1.1 copy-done.1
  1.9 23.8 %place_beams.1 = (f32[4,32,192,128]{3,2,1,0:T(8,128)}, f32[4,9,24,128]{3,2,1,0:T(8,128)S(1)}) custom-call(s32[2]{0:T(128)S(1)} %pad_add_fusion.where_ref, s32[9,2]{1,0:T(8,128)S(1)} %copy.6.offsets_ref, f32[32,9,128,128]{3,2,1,0:T(8,128)} %image_ref.1, f32[9,128,128]{2,1,0:T(8,128)S(1)} %copy-done.1), custom_call_target="tpu_custom_call" | custom-call | tf_op jit(solution)/shard_map/place_beams/pallas_call | solution.py:118
  25.7 0.0 copy-start.2
  25.7 0.8 copy-done.2
  26.5 0.0 copy-start.4
  26.5 186.7 %exchange.1 = (f32[256,24,128]{2,1,0:T(8,128)}, s32[256,24,128]{2,1,0:T(8,128)}, f32[36,24,128]{2,1,0:T(8,128)}) custom-call(f32[4,32,192,128]{3,2,1,0:T(8,128)} %get-tuple-element.10.sums_ref, s32[32,8,24,128]{3,2,1,0:T(8,128)} %bitcast.4, f32[4,9,24,128]{3,2,1,0:T(8,128)} %copy-done.2), custom_call_target="tpu_custom_call" | custom-call | tf_op jit(solution)/shard_map/exchange/pallas_call | solution.py:365
  213.2 0.0 copy-done.4
  213.2 0.0 copy-start
  213.2 1.9 copy-done
  215.1 0.0 copy-start.3
  215.1 1.0 copy-done.3
  216.1 14.2 %fit.1 = f32[256,24,128]{2,1,0:T(8,128)} custom-call(s32[1]{0:T(128)} %bitcast.where_ref, s32[256]{0:T(256)S(1)} %copy-done.4, f32[256,24,128]{2,1,0:T(8,128)S(1)} %copy-done, s32[256,24,128]{2,1,0:T(8,128)} %get-tuple-element.13.flag_ref, f32[36,24,128]{2,1,0:T(8,128)S(1)} %copy-done.3), custom_call_target="tpu_custom_call" | custom-call | tf_op jit(solution)/shard_map/fit/pallas_call | solution.py:531
Async XLA Ops:
  0.8 1.1 copy-start.1
  25.7 0.8 copy-start.2
  26.5 186.7 %copy-start.4 = (s32[256]{0:T(256)S(1)}, s32[256]{0:T(256)}, u32[]{:S(2)}) copy-start(s32[256]{0:T(256)} %regression_ref.1) | copy-start | bytes 3076
  213.2 1.9 copy-start
  215.1 1.0 copy-start.3

commit v3 on v2

--- a/solution.py
+++ b/solution.py
@@ -13,6 +13,8 @@
 JITTER = 16
 LANES = 128
 OUTSIDE = -1.0e4
+PAD = 40
+SLOTS = 3
 MESH = pl.DeviceIdType.MESH
 
 
@@ -36,122 +38,72 @@
     return first // 8 * 8, min(MOS_ROWS, -(-last // 8) * 8)
 
 
-def place_kernel(
-    where_ref, offsets_ref, image_ref, weight_ref, sums_ref, tiles_ref, log_ref, plane_ref, *, slope
-):
-    step = pl.program_id(0)
-    blocks, depth, _, _ = sums_ref.shape
-    beams, side, _ = weight_ref.shape
-    tile_rows = tiles_ref.shape[2]
+def tiles_kernel(where_ref, offsets_ref, weight_ref, tiles_ref, plane_ref):
+    blocks, beams, tile_rows, _ = tiles_ref.shape
+    side = weight_ref.shape[1]
     piece = 64
     lane = lax.broadcasted_iota(jnp.int32, (piece, LANES), 1)
 
-    def corner(beam):
+    def spread(beam, carry):
         row, col = offsets_ref[beam, 0], offsets_ref[beam, 1]
-        return row, lax.shift_right_logical(col, 7), jnp.bitwise_and(col, LANES - 1)
-
-    @pl.when(step == 0)
-    def _():
-        log_ref[...] = jnp.log(weight_ref[...])
-
-        def spread(beam, carry):
-            row, block, shift = corner(beam)
-            plane_ref[...] = jnp.full(plane_ref.shape, OUTSIDE, jnp.float32)
-
-            def part(index, inner):
-                start = pl.multiple_of(index * piece, piece)
-                value = pltpu.roll(log_ref[beam, pl.ds(start, piece), :], shift, 1)
-                plane_ref[block, pl.ds(row + start, piece), :] = jnp.where(
-                    lane >= shift, value, OUTSIDE
-                )
-
-                @pl.when(block < blocks - 1)
-                def _():
-                    plane_ref[block + 1, pl.ds(row + start, piece), :] = jnp.where(
-                        lane < shift, value, OUTSIDE
-                    )
-
-                return inner
-
-            lax.fori_loop(0, side // piece, part, 0)
-            tiles_ref[:, beam, :, :] = plane_ref[:, pl.ds(where_ref[1], tile_rows), :]
-            return carry
-
-        lax.fori_loop(0, beams, spread, 0)
-
-    sums_ref[...] = jnp.zeros(sums_ref.shape, jnp.float32)
-    exponent = 1.0 + slope * (where_ref[0] + step * depth).astype(jnp.float32)
-
-    def add_beam(beam, carry):
-        row, block, shift = corner(beam)
-        after = jnp.minimum(block + 1, blocks - 1)
+        block, shift = lax.shift_right_logical(col, 7), jnp.bitwise_and(col, LANES - 1)
+        plane_ref[...] = jnp.full(plane_ref.shape, OUTSIDE, jnp.float32)
 
         def part(index, inner):
             start = pl.multiple_of(index * piece, piece)
-            rows = pl.ds(row + start, piece)
-            logs = log_ref[beam, pl.ds(start, piece), :]
-            response = jnp.exp(exponent * logs)
-            ratio = jnp.exp(slope * logs)
-            values = []
-            for channel in range(depth):
-                value = image_ref[channel, beam, pl.ds(start, piece), :] * response
-                values.append(pltpu.roll(value, shift, 1))
-                response = response * ratio
-            for target, inside in ((block, lane >= shift), (after, lane < shift)):
-                sums = [
-                    sums_ref[target, channel, rows, :] + jnp.where(inside, value, 0.0)
-                    for channel, value in enumerate(values)
-                ]
-                for channel, value in enumerate(sums):
-                    sums_ref[target, channel, rows, :] = value
+            value = jnp.log(weight_ref[beam, pl.ds(start, piece), :])
+            value = pltpu.roll(value, shift, 1)
+            plane_ref[block, pl.ds(row + start, piece), :] = jnp.where(
+                lane >= shift, value, OUTSIDE
+            )
+
+            @pl.when(block < blocks - 1)
+            def _():
+                plane_ref[block + 1, pl.ds(row + start, piece), :] = jnp.where(
+                    lane < shift, value, OUTSIDE
+                )
+
             return inner
 
         lax.fori_loop(0, side // piece, part, 0)
+        tiles_ref[:, beam, :, :] = plane_ref[:, pl.ds(where_ref[0], tile_rows), :]
         return carry
 
-    lax.fori_loop(0, beams, add_beam, 0)
-
-
-def place(where, offsets, images, beam_weight, blocks, tile_rows, channels):
-    ch_dev, beams, side, _ = images.shape
-    depth = 4
+    lax.fori_loop(0, beams, spread, 0)
+
+
+def log_tiles(where, offsets, beam_weight, blocks, tile_rows):
+    beams = beam_weight.shape[0]
+    smem = pl.BlockSpec(memory_space=pltpu.SMEM)
+    vmem = pl.BlockSpec(memory_space=pltpu.VMEM)
     return pl.pallas_call(
-        functools.partial(place_kernel, slope=0.5 / (channels - 1)),
-        grid=(ch_dev // depth,),
-        in_specs=[
-            pl.BlockSpec(memory_space=pltpu.SMEM),
-            pl.BlockSpec(memory_space=pltpu.SMEM),
-            pl.BlockSpec((depth, beams, side, side), lambda s: (s, 0, 0, 0)),
-            pl.BlockSpec((beams, side, side), lambda s: (0, 0, 0)),
-        ],
-        out_specs=[
-            pl.BlockSpec((blocks, depth, MOS_ROWS, LANES), lambda s: (0, s, 0, 0)),
-            pl.BlockSpec((blocks, beams, tile_rows, LANES), lambda s: (0, 0, 0, 0)),
-        ],
-        out_shape=[
-            jax.ShapeDtypeStruct((blocks, ch_dev, MOS_ROWS, LANES), jnp.float32),
-            jax.ShapeDtypeStruct((blocks, beams, tile_rows, LANES), jnp.float32),
-        ],
-        scratch_shapes=[
-            pltpu.VMEM((beams, side, side), jnp.float32),
-            pltpu.VMEM((blocks, MOS_ROWS, LANES), jnp.float32),
-        ],
-        compiler_params=pltpu.CompilerParams(vmem_limit_bytes=48 << 20),
-        name="place_beams",
-    )(where, offsets, images, beam_weight)
+        tiles_kernel,
+        in_specs=[smem, smem, vmem],
+        out_specs=vmem,
+        out_shape=jax.ShapeDtypeStruct((blocks, beams, tile_rows, LANES), jnp.float32),
+        scratch_shapes=[pltpu.VMEM((blocks, MOS_ROWS, LANES), jnp.float32)],
+        name="log_tiles",
+    )(where, offsets, beam_weight)
 
 
 def exchange_kernel(
-    sums_ref,
+    offsets_ref,
+    weight_ref,
+    image_ref,
     flags_ref,
     logs_ref,
     sky_out,
     flag_out,
-    log_out,
+    total_out,
     own,
     up,
     down,
     rowed,
+    fetched,
+    own_logs,
+    padded,
+    arrived,
+    total,
     own_sem,
     keep_sem,
     up_recv,
@@ -170,13 +122,16 @@
     depth,
     reach_up,
     reach_down,
+    slope,
 ):
     group = lax.axis_index("beam")
     tile = lax.axis_index("chan")
-    ch_dev = sums_ref.shape[1]
+    ch_dev = image_ref.shape[0]
+    side = weight_ref.shape[1]
     tile_rows = flags_ref.shape[2]
     beams = logs_ref.shape[1]
     steps = ch_dev // depth
+    run = tiles * depth
 
     others = [lax.rem(tile + k, tiles) for k in range(1, tiles)]
     columns = [lax.rem(group + k, groups) for k in range(1, groups)]
@@ -188,19 +143,18 @@
         pl.semaphore_signal(barrier, inc=1, device_id={"beam": other}, device_id_type=MESH)
 
     def load(step):
-        span = pl.ds(step * depth, depth)
-        return pltpu.make_async_copy(sums_ref.at[:, span], own.at[:, span], own_sem.at[step])
-
-    def fetch(step, carry):
+        slot = lax.rem(step, SLOTS)
+        return pltpu.make_async_copy(
+            image_ref.at[pl.ds(step * depth, depth)], fetched.at[slot], own_sem.at[slot]
+        )
+
+    for step in range(min(SLOTS, steps)):
         load(step).start()
-        return carry
-
-    lax.fori_loop(0, steps, fetch, 0)
     mine = pl.ds(tile * ch_dev, ch_dev)
     kept = [
         pltpu.make_async_copy(flags_ref.at[:, tile], flag_out.at[mine], keep_sem.at[0]),
         pltpu.make_async_copy(
-            logs_ref.at[group], log_out.at[pl.ds(group * beams, beams)], keep_sem.at[1]
+            logs_ref.at[group], arrived.at[pl.ds(group * beams, beams)], keep_sem.at[1]
         ),
     ]
     for copy in kept:
@@ -212,7 +166,7 @@
         small.append(
             pltpu.make_async_remote_copy(
                 src_ref=logs_ref.at[other],
-                dst_ref=log_out.at[pl.ds(group * beams, beams)],
+                dst_ref=arrived.at[pl.ds(group * beams, beams)],
                 send_sem=log_send.at[k],
                 recv_sem=log_recv.at[k],
                 device_id={"beam": other},
@@ -232,6 +186,76 @@
         )
     for copy in small:
         copy.start()
+
+    own_logs[...] = jnp.log(weight_ref[...])
+    padded[...] = jnp.zeros(padded.shape, jnp.float32)
+    lane = lax.broadcasted_iota(jnp.int32, (1, LANES), 1)
+
+    def place(z, step):
+        load(step).wait()
+        slot = lax.rem(step, SLOTS)
+        exponent = 1.0 + slope * (tile * ch_dev + step * depth).astype(jnp.float32)
+
+        def weigh(beam, carry):
+            logs = own_logs[beam]
+            response = jnp.exp(exponent * logs)
+            ratio = jnp.exp(slope * logs)
+            for channel in range(depth):
+                padded[channel, beam, PAD : PAD + side, :] = (
+                    fetched[slot, channel, beam] * response
+                )
+                response = response * ratio
+            return carry
+
+        lax.fori_loop(0, beams, weigh, 0)
+
+        @pl.when(step + SLOTS < steps)
+        def _():
+            load(step + SLOTS).start()
+
+        span = pl.ds(step * depth, depth)
+        own[:, span] = jnp.zeros((groups, depth, MOS_ROWS, LANES), jnp.float32)
+        for beam in range(beams):
+            place_row, place_col = divmod(z * beams + beam, GRID)
+            low, high = start_range(place_row, MOS_ROWS - side)
+            first, last = low // 8 * 8, -(-(high + side) // 8) * 8
+            row = jnp.clip(offsets_ref[beam, 0], low, high)
+            low, high = start_range(place_col, MOS_COLS - side)
+            block = low // LANES
+            values = [
+                padded[channel, beam, pl.ds(PAD + first - row, last - first), :]
+                for channel in range(depth)
+            ]
+            if low == high and low % LANES == 0:
+                for channel, value in enumerate(values):
+                    own[block, step * depth + channel, first:last, :] += value
+                continue
+            shift = jnp.clip(offsets_ref[beam, 1], low, high) - block * LANES
+            values = [pltpu.roll(value, shift, 1) for value in values]
+            for target, inside in ((block, lane >= shift), (block + 1, lane < shift)):
+                for channel, value in enumerate(values):
+                    own[target, step * depth + channel, first:last, :] += jnp.where(
+                        inside, value, 0.0
+                    )
+
+    def add_weights(z, step):
+        start = step * run
+        exponent = 1.0 + slope * start.astype(jnp.float32)
+        piece = 8 if tile_rows % 8 == 0 else tile_rows
+        for part in range(tile_rows // piece):
+            rows = pl.ds(part * piece, piece)
+            sums = [jnp.zeros((piece, LANES), jnp.float32)] * run
+            for place_row in range(GRID):
+                for place_col in range(z, z + 3):
+                    logs = arrived[place_row * GRID + place_col, rows, :]
+                    value = jnp.exp((2.0 * exponent) * logs)
+                    ratio = jnp.exp((2.0 * slope) * logs)
+                    for k in range(run):
+                        sums[k] = sums[k] + value
+                        if k < run - 1:
+                            value = value * ratio
+            for k in range(run):
+                total[start + k, rows, :] = sums[k]
 
     def up_copy(z, block, step):
         span, rows = pl.ds(step * depth, depth), pl.ds(0, reach_up[z, block])
@@ -318,13 +342,23 @@
             def work(turn, carry):
                 @pl.when(turn < steps)
                 def _():
-                    load(turn).wait()
+                    place(z, turn)
 
                 for lag, act in ((up_lag, pass_up), (down_lag, pass_down), (last_lag, finish)):
 
                     @pl.when(jnp.logical_and(turn >= lag, turn < steps + lag))
                     def _(lag=lag, act=act):
                         act(turn - lag)
+
+                @pl.when(turn == 1)
+                def _():
+                    for copy in small[: groups - 1]:
+                        copy.wait()
+                    kept[1].wait()
+
+                @pl.when(jnp.logical_and(turn >= 1, turn < steps + 1))
+                def _():
+                    add_weights(z, turn - 1)
 
                 return carry
 
@@ -337,23 +371,27 @@
                 ref = down.at[block, :, pl.ds(first, MOS_ROWS - first)]
                 pltpu.make_async_copy(ref, ref, down_send.at[block]).wait()
 
-    kept.append(pltpu.make_async_copy(rowed.at[tile], sky_out.at[mine], keep_sem.at[2]))
-    kept[-1].start()
-    for copy in small:
+    last = [
+        pltpu.make_async_copy(rowed.at[tile], sky_out.at[mine], keep_sem.at[2]),
+        pltpu.make_async_copy(total, total_out, keep_sem.at[3]),
+        kept[0],
+    ]
+    for copy in last[:2]:
+        copy.start()
+    for copy in small[groups - 1 :]:
         copy.wait()
     for k, other in enumerate(others):
         sky_copy(k, other, pl.ds(0, ch_dev)).wait()
-    for copy in kept:
+    for copy in last:
         copy.wait()
 
 
-def exchange(sums, flags, logs, groups, tiles):
-    ch_dev = sums.shape[1]
+def exchange(offsets, beam_weight, images, flags, logs, groups, tiles):
+    ch_dev, _, side, _ = images.shape
     tile_rows = flags.shape[2]
     beams = logs.shape[1]
     depth = 2
     steps = ch_dev // depth
-    side = MOS_ROWS - start_range(GRID - 1, MOS_ROWS - LANES)[0]
     reach_up, reach_down = {}, {}
     for block in range(groups):
         rows = [covered_rows(group, beams, side, block) for group in range(groups)]
@@ -370,21 +408,33 @@
             depth=depth,
             reach_up=reach_up,
             reach_down=reach_down,
+            slope=0.5 / (tiles * ch_dev - 1),
         ),
-        in_specs=[any_space] * 3,
+        in_specs=[
+            pl.BlockSpec(memory_space=pltpu.SMEM),
+            pl.BlockSpec(memory_space=pltpu.VMEM),
+            any_space,
+            any_space,
+            any_space,
+        ],
         out_specs=[any_space] * 3,
         out_shape=[
             jax.ShapeDtypeStruct((tiles * ch_dev, tile_rows, LANES), jnp.float32),
             jax.ShapeDtypeStruct((tiles * ch_dev, tile_rows, LANES), jnp.int32),
-            jax.ShapeDtypeStruct((groups * beams, tile_rows, LANES), jnp.float32),
+            jax.ShapeDtypeStruct((tiles * ch_dev, tile_rows, LANES), jnp.float32),
         ],
         scratch_shapes=[
             pltpu.VMEM((groups, ch_dev, MOS_ROWS, LANES), jnp.float32),
             pltpu.VMEM((groups - 1, ch_dev, MOS_ROWS, LANES), jnp.float32),
             pltpu.VMEM((groups - 1, ch_dev, MOS_ROWS, LANES), jnp.float32),
             pltpu.VMEM((tiles, ch_dev, tile_rows, LANES), jnp.float32),
-            dma((steps,)),
-            dma((3,)),
+            pltpu.VMEM((SLOTS, depth, beams, side, side), jnp.float32),
+            pltpu.VMEM((beams, side, side), jnp.float32),
+            pltpu.VMEM((depth, beams, PAD + side + PAD, side), jnp.float32),
+            pltpu.VMEM((groups * beams, tile_rows, LANES), jnp.float32),
+            pltpu.VMEM((tiles * ch_dev, tile_rows, LANES), jnp.float32),
+            dma((SLOTS,)),
+            dma((4,)),
             dma((steps, groups)),
             dma((steps, groups)),
             dma((groups,)),
@@ -400,7 +450,7 @@
             collective_id=0, has_side_effects=True, vmem_limit_bytes=56 << 20
         ),
         name="exchange",
-    )(sums, flags, logs)
+    )(offsets, beam_weight, images, flags, logs)
 
 
 def solve_cubic(normal_matrix, right_side):
@@ -437,32 +487,8 @@
 )
 
 
-def fit_kernel(where_ref, regression_ref, sky_ref, flag_ref, log_ref, out_ref, total_ref, *, slope):
+def fit_kernel(regression_ref, sky_ref, flag_ref, weights_ref, out_ref, total_ref):
     channels, rows, _ = sky_ref.shape
-    piece = 8 if rows % 8 == 0 else rows
-    run = 16
-    first = where_ref[0]
-    beams = [(r * GRID, q) for r in range(GRID) for q in range(3)]
-
-    def totals(index, carry):
-        start = index * run
-        exponent = 1.0 + slope * start.astype(jnp.float32)
-        for part in range(rows // piece):
-            span = pl.ds(part * piece, piece)
-            total = [jnp.zeros((piece, LANES), jnp.float32)] * run
-            for begin, q in beams:
-                logs = log_ref[begin + q + first, span, :]
-                value = jnp.exp((2.0 * exponent) * logs)
-                ratio = jnp.exp((2.0 * slope) * logs)
-                for k in range(run):
-                    total[k] = total[k] + value
-                    if k < run - 1:
-                        value = value * ratio
-            for k in range(run):
-                total_ref[start + k, span, :] = total[k]
-        return carry
-
-    lax.fori_loop(0, channels // run, totals, 0)
 
     def position(channel):
         return (2.0 * channel.astype(jnp.float32) + 1.0) * (1.0 / channels) - 1.0
@@ -471,7 +497,7 @@
         powers, rights = list(carry[:7]), list(carry[7:])
         x = position(channel)
         open_sky = 1.0 - flag_ref[channel].astype(jnp.float32)
-        total = total_ref[channel]
+        total = weights_ref[channel]
         sky = open_sky * sky_ref[channel] / total
         total_ref[channel] = sky
         chosen = regression_ref[channel].astype(jnp.float32)
@@ -524,34 +550,30 @@
     out_ref[channels - 1] = 0.25 * before + 0.5 * here
 
 
-def fit(where, regression, sky, flags, logs):
-    channels = sky.shape[0]
+def fit(regression, sky, flags, total):
     smem = pl.BlockSpec(memory_space=pltpu.SMEM)
     vmem = pl.BlockSpec(memory_space=pltpu.VMEM)
     return pl.pallas_call(
-        functools.partial(fit_kernel, slope=0.5 / (channels - 1)),
-        in_specs=[smem, smem, vmem, vmem, vmem],
+        fit_kernel,
+        in_specs=[smem, vmem, vmem, vmem],
         out_specs=vmem,
         out_shape=jax.ShapeDtypeStruct(sky.shape, jnp.float32),
         scratch_shapes=[pltpu.VMEM(sky.shape, jnp.float32)],
         compiler_params=pltpu.CompilerParams(vmem_limit_bytes=48 << 20),
         name="fit",
-    )(where, regression, sky, flags, logs)
+    )(regression, sky, flags, total)
 
 
 def local(
     images, beam_weight, offsets, rejected_indicator, regression_indicator, *, groups, tiles
 ):
     ch_dev = images.shape[0]
-    channels = regression_indicator.shape[0]
     tile_rows = MOS_ROWS // tiles
-    tile = lax.axis_index("chan")
-    group = lax.axis_index("beam")
-    where = jnp.stack([tile * ch_dev, tile * tile_rows]).astype(jnp.int32)
-    sums, logs = place(where, offsets, images, beam_weight, groups, tile_rows, channels)
+    where = (lax.axis_index("chan") * tile_rows).astype(jnp.int32)[None]
+    logs = log_tiles(where, offsets, beam_weight, groups, tile_rows)
     flags = rejected_indicator.reshape(ch_dev, tiles, tile_rows, rejected_indicator.shape[2])
-    sky, flags, logs = exchange(sums, flags, logs, groups, tiles)
-    return fit(group[None].astype(jnp.int32), regression_indicator, sky, flags, logs)
+    sky, flags, total = exchange(offsets, beam_weight, images, flags, logs, groups, tiles)
+    return fit(regression_indicator, sky, flags, total)
 
 
 def solution(mesh):

time: 231 us -> 206 us (0.89)
  Pallas kernels: 225 us -> 202 us
    pallas_call x2, Pallas kernels: 38 us -> 14.5 us  [the longest x1 10.8 us: fit(): pl.pallas_call(fit_kernel, in_specs=[smem, vmem, vmem, vmem], out_specs=v...]
    unnamed x11 -> x5, local copies, waits for them, and re-layouts: 5.49 us -> 3.24 us
where the time goes in v3:
time: 206 us
  Pallas kernels  202 us (98%)
  local copies, waits for them, and re-layouts  3.24 us (2%)
    pallas_call x1, Pallas kernels, exchange(): pl.pallas_call(functools.partial(exchange_kernel, groups=groups, tiles=ti...  188 us
    pallas_call x1, Pallas kernels, fit(): pl.pallas_call(fit_kernel, in_specs=[smem, vmem, vmem, vmem], out_specs=v...  10.8 us

profile of v3, /device:TPU:0, one launch (start us, length us, event | category | flops | bytes accessed | tf_op | source)
XLA Modules:
  0.0 205.5 jit_solution(16642811374489308124)
XLA Ops:
  0.0 1.4 copy.7.offsets_ref
  1.4 3.6 %log_tiles.1.logs_ref = f32[4,9,24,128]{3,2,1,0:T(8,128)} custom-call(s32[1]{0:T(128)} %bitcast.1.where_ref, s32[9,2]{1,0:T(8,128)} %copy.7.offsets_ref, f32[9,128,128]{2,1,0:T(8,128)} %weight_ref.3), custom_call_target="tpu_custom_call" | custom-call | tf_op jit(solution)/shard_map/log_tiles/pallas_call | solution.py:79
  5.0 0.0 copy-start.1
  5.0 187.8 %exchange.1 = (f32[256,24,128]{2,1,0:T(8,128)}, s32[256,24,128]{2,1,0:T(8,128)}, f32[256,24,128]{2,1,0:T(8,128)}) custom-call(s32[9,2]{1,0:T(8,128)} %copy.7.offsets_ref, f32[9,128,128]{2,1,0:T(8,128)} %weight_ref.3, f32[32,9,128,128]{3,2,1,0:T(8,128)} %image_ref.1, s32[32,8,24,128]{3,2,1,0:T(8,128)} %bitcast.2, f32[4,9,24,128]{3,2,1,0:T(8,128)} %log_tiles.1.logs_ref), custom_call_target="tpu_custom_call" | custom-call | tf_op jit(solution)/shard_map/exchange/pallas_call | solution.py:403
  192.8 0.0 copy-done.1
  192.8 0.0 copy-start
  192.8 1.9 copy-done
  194.7 10.8 %fit.1 = f32[256,24,128]{2,1,0:T(8,128)} custom-call(s32[256]{0:T(256)S(1)} %copy-done.1, f32[256,24,128]{2,1,0:T(8,128)S(1)} %copy-done, s32[256,24,128]{2,1,0:T(8,128)} %get-tuple-element.9.flag_ref, f32[256,24,128]{2,1,0:T(8,128)} %get-tuple-element.10.weights_ref), custom_call_target="tpu_custom_call" | custom-call | tf_op jit(solution)/shard_map/fit/pallas_call | solution.py:556
Async XLA Ops:
  5.0 187.8 %copy-start.1 = (s32[256]{0:T(256)S(1)}, s32[256]{0:T(256)}, u32[]{:S(2)}) copy-start(s32[256]{0:T(256)} %regression_ref.1) | copy-start | bytes 3076
  192.8 1.9 copy-start

commit v4 on v3

--- a/solution.py
+++ b/solution.py
@@ -36,6 +36,29 @@
         low, high = start_range(beam // GRID, MOS_ROWS - side)
         first, last = min(first, low), max(last, high + side)
     return first // 8 * 8, min(MOS_ROWS, -(-last // 8) * 8)
+
+
+def reaching(group, beams_each, side, block):
+    found = []
+    for place in range(beams_each):
+        low, high = start_range((group * beams_each + place) % GRID, MOS_COLS - side)
+        if high + side > block * LANES and low < (block + 1) * LANES:
+            found.append(place)
+    return found
+
+
+def foldable(group, beams_each, side, block, upward):
+    if block == group:
+        return False
+    for place in reaching(group, beams_each, side, block):
+        beam = group * beams_each + place
+        low, high = start_range(beam // GRID, MOS_ROWS - side)
+        left, right = start_range(beam % GRID, MOS_COLS - side)
+        if upward and high > 0 and right + side - block * LANES > LANES // 2:
+            return False
+        if not upward and low < MOS_ROWS - side and left - block * LANES < LANES // 2:
+            return False
+    return True
 
 
 def tiles_kernel(where_ref, offsets_ref, weight_ref, tiles_ref, plane_ref):
@@ -122,6 +145,8 @@
     depth,
     reach_up,
     reach_down,
+    fold_up,
+    fold_down,
     slope,
 ):
     group = lax.axis_index("beam")
@@ -161,18 +186,17 @@
         copy.start()
     pl.semaphore_wait(barrier, len(others) + len(columns))
 
+    def log_copy(source, k, beam):
+        return pltpu.make_async_remote_copy(
+            src_ref=logs_ref.at[(source + k) % groups, beam],
+            dst_ref=arrived.at[source * beams + beam],
+            send_sem=log_send.at[k - 1],
+            recv_sem=log_recv.at[k - 1],
+            device_id={"beam": (source + k) % groups},
+            device_id_type=MESH,
+        )
+
     small = []
-    for k, other in enumerate(columns):
-        small.append(
-            pltpu.make_async_remote_copy(
-                src_ref=logs_ref.at[other],
-                dst_ref=arrived.at[pl.ds(group * beams, beams)],
-                send_sem=log_send.at[k],
-                recv_sem=log_recv.at[k],
-                device_id={"beam": other},
-                device_id_type=MESH,
-            )
-        )
     for k, other in enumerate(others):
         small.append(
             pltpu.make_async_remote_copy(
@@ -245,9 +269,9 @@
         for part in range(tile_rows // piece):
             rows = pl.ds(part * piece, piece)
             sums = [jnp.zeros((piece, LANES), jnp.float32)] * run
-            for place_row in range(GRID):
-                for place_col in range(z, z + 3):
-                    logs = arrived[place_row * GRID + place_col, rows, :]
+            for source in range(groups):
+                for beam in reaching(source, beams, side, z):
+                    logs = arrived[source * beams + beam, rows, :]
                     value = jnp.exp((2.0 * exponent) * logs)
                     ratio = jnp.exp((2.0 * slope) * logs)
                     for k in range(run):
@@ -256,6 +280,29 @@
                             value = value * ratio
             for k in range(run):
                 total[start + k, rows, :] = sums[k]
+
+    def unfold_up(z, block, span):
+        last = reach_up[z - 1, block]
+        if z != 1 or block not in fold_up:
+            return last
+        half = last - side
+        both = up[block - 1, span, side:last, :]
+        up[block - 1, span, side:last, :] = jnp.where(lane < LANES // 2, both, 0.0)
+        up[block - 1, span, last : last + half, :] = pltpu.roll(
+            jnp.where(lane < LANES // 2, 0.0, both), LANES // 2, 2
+        )
+        return last + half
+
+    def unfold_down(z, block, span):
+        first, edge = reach_down[z + 1, block], MOS_ROWS - side
+        if z != groups - 2 or block not in fold_down:
+            return first
+        both = down[block, span, first:edge, :]
+        down[block, span, first:edge, :] = jnp.where(lane < LANES // 2, 0.0, both)
+        down[block, span, 2 * first - edge : first, :] = pltpu.roll(
+            jnp.where(lane < LANES // 2, both, 0.0), LANES // 2, 2
+        )
+        return 2 * first - edge
 
     def up_copy(z, block, step):
         span, rows = pl.ds(step * depth, depth), pl.ds(0, reach_up[z, block])
@@ -296,6 +343,9 @@
 
         @pl.when(group == z)
         def _(z=z):
+            for k in range(1, groups):
+                for beam in reaching(z, beams, side, (z + k) % groups):
+                    log_copy(z, k, beam).start()
             lower = 2 * z < groups
             up_lag, down_lag = (0, 2) if lower else (2, 0)
             last_lag = 6 if z in (0, groups - 1) else 3
@@ -304,33 +354,43 @@
                 span = pl.ds(step * depth, depth)
                 for block in range(groups - 1, z, -1):
                     if z > 0:
-                        old, new = reach_up[z - 1, block], reach_up[z, block]
                         up_copy(z - 1, block, step).wait_recv()
+                        old, new = unfold_up(z, block, span), reach_up[z, block]
                         up[block - 1, span, 0:old, :] += own[block, span, 0:old, :]
                         if new > old:
                             up[block - 1, span, old:new, :] = own[block, span, old:new, :]
+                    elif block in fold_up:
+                        last = reach_up[z, block]
+                        own[block, span, side:last, :] += pltpu.roll(
+                            own[block, span, last : 2 * last - side, :], LANES // 2, 2
+                        )
                     up_copy(z, block, step).start()
 
             def pass_down(step):
                 span = pl.ds(step * depth, depth)
                 for block in range(z):
                     if z < groups - 1:
-                        old, new = reach_down[z + 1, block], reach_down[z, block]
                         down_copy(z + 1, block, step).wait_recv()
+                        old, new = unfold_down(z, block, span), reach_down[z, block]
                         down[block, span, old:, :] += own[block, span, old:, :]
                         if new < old:
                             down[block, span, new:old, :] = own[block, span, new:old, :]
+                    elif block in fold_down:
+                        first, edge = reach_down[z, block], MOS_ROWS - side
+                        own[block, span, first:edge, :] += pltpu.roll(
+                            own[block, span, 2 * first - edge : first, :], LANES // 2, 2
+                        )
                     down_copy(z, block, step).start()
 
             def finish(step):
                 span = pl.ds(step * depth, depth)
                 if z > 0:
-                    old = reach_up[z - 1, z]
                     up_copy(z - 1, z, step).wait_recv()
+                    old = unfold_up(z, z, span)
                     own[z, span, 0:old, :] += up[z - 1, span, 0:old, :]
                 if z < groups - 1:
-                    old = reach_down[z + 1, z]
                     down_copy(z + 1, z, step).wait_recv()
+                    old = unfold_down(z, z, span)
                     own[z, span, old:, :] += down[z, span, old:, :]
                 for index in range(tiles):
                     rowed[index, span, :, :] = own[
@@ -352,9 +412,16 @@
 
                 @pl.when(turn == 1)
                 def _():
-                    for copy in small[: groups - 1]:
-                        copy.wait()
                     kept[1].wait()
+                    for k in range(1, groups):
+                        count = len(reaching(z, beams, side, (z + k) % groups))
+                        ref = arrived.at[pl.ds(0, count)]
+                        if count:
+                            pltpu.make_async_copy(ref, ref, log_send.at[k - 1]).wait()
+                        count = len(reaching((z - k) % groups, beams, side, z))
+                        ref = arrived.at[pl.ds(0, count)]
+                        if count:
+                            pltpu.make_async_copy(ref, ref, log_recv.at[k - 1]).wait()
 
                 @pl.when(jnp.logical_and(turn >= 1, turn < steps + 1))
                 def _():
@@ -378,7 +445,7 @@
     ]
     for copy in last[:2]:
         copy.start()
-    for copy in small[groups - 1 :]:
+    for copy in small:
         copy.wait()
     for k, other in enumerate(others):
         sky_copy(k, other, pl.ds(0, ch_dev)).wait()
@@ -398,6 +465,17 @@
         for z in range(groups):
             reach_up[z, block] = max(high for _, high in rows[: z + 1])
             reach_down[z, block] = min(low for low, _ in rows[z:])
+    fold_up, fold_down = [], []
+    edge = MOS_ROWS - side
+    for block in range(groups):
+        extra = reach_up[0, block] - side
+        if extra > 0 and extra % 16 == 0 and foldable(0, beams, side, block, True):
+            fold_up.append(block)
+            reach_up[0, block] = side + extra // 2
+        extra = edge - reach_down[groups - 1, block]
+        if extra > 0 and extra % 16 == 0 and foldable(groups - 1, beams, side, block, False):
+            fold_down.append(block)
+            reach_down[groups - 1, block] = edge - extra // 2
     dma = pltpu.SemaphoreType.DMA
     any_space = pl.BlockSpec(memory_space=pl.ANY)
     return pl.pallas_call(
@@ -408,6 +486,8 @@
             depth=depth,
             reach_up=reach_up,
             reach_down=reach_down,
+            fold_up=fold_up,
+            fold_down=fold_down,
             slope=0.5 / (tiles * ch_dev - 1),
         ),
         in_specs=[

time: 206 us -> 196 us (0.951)
  Pallas kernels: 202 us -> 193 us
    pallas_call x1, Pallas kernels: 188 us -> 178 us  [exchange(): pl.pallas_call(functools.partial(exchange_kernel, groups=groups, tiles=ti...]
where the time goes in v4:
time: 196 us
  Pallas kernels  193 us (98%)
  local copies, waits for them, and re-layouts  3.24 us (2%)
    pallas_call x1, Pallas kernels, exchange(): pl.pallas_call(functools.partial(exchange_kernel, groups=groups, tiles=ti...  178 us
    pallas_call x1, Pallas kernels, fit(): pl.pallas_call(fit_kernel, in_specs=[smem, vmem, vmem, vmem], out_specs=v...  10.8 us

profile of v4, /device:TPU:0, one launch (start us, length us, event | category | flops | bytes accessed | tf_op | source)
XLA Modules:
  0.0 195.9 jit_solution(10148940686734912538)
XLA Ops:
  0.0 1.4 copy.7.offsets_ref
  1.4 3.6 %log_tiles.1.logs_ref = f32[4,9,24,128]{3,2,1,0:T(8,128)} custom-call(s32[1]{0:T(128)} %bitcast.1.where_ref, s32[9,2]{1,0:T(8,128)} %copy.7.offsets_ref, f32[9,128,128]{2,1,0:T(8,128)} %weight_ref.3), custom_call_target="tpu_custom_call" | custom-call | tf_op jit(solution)/shard_map/log_tiles/pallas_call | solution.py:102
  5.0 0.0 copy-start.1
  5.0 178.2 %exchange.1 = (f32[256,24,128]{2,1,0:T(8,128)}, s32[256,24,128]{2,1,0:T(8,128)}, f32[256,24,128]{2,1,0:T(8,128)}) custom-call(s32[9,2]{1,0:T(8,128)} %copy.7.offsets_ref, f32[9,128,128]{2,1,0:T(8,128)} %weight_ref.3, f32[32,9,128,128]{3,2,1,0:T(8,128)} %image_ref.1, s32[32,8,24,128]{3,2,1,0:T(8,128)} %bitcast.2, f32[4,9,24,128]{3,2,1,0:T(8,128)} %log_tiles.1.logs_ref), custom_call_target="tpu_custom_call" | custom-call | tf_op jit(solution)/shard_map/exchange/pallas_call | solution.py:481
  183.1 0.0 copy-done.1
  183.1 0.0 copy-start
  183.2 1.9 copy-done
  185.0 10.8 %fit.1 = f32[256,24,128]{2,1,0:T(8,128)} custom-call(s32[256]{0:T(256)S(1)} %copy-done.1, f32[256,24,128]{2,1,0:T(8,128)S(1)} %copy-done, s32[256,24,128]{2,1,0:T(8,128)} %get-tuple-element.9.flag_ref, f32[256,24,128]{2,1,0:T(8,128)} %get-tuple-element.10.weights_ref), custom_call_target="tpu_custom_call" | custom-call | tf_op jit(solution)/shard_map/fit/pallas_call | solution.py:636
Async XLA Ops:
  5.0 178.2 %copy-start.1 = (s32[256]{0:T(256)S(1)}, s32[256]{0:T(256)}, u32[]{:S(2)}) copy-start(s32[256]{0:T(256)} %regression_ref.1) | copy-start | bytes 3076
  183.1 1.9 copy-start

commit v5 on v4

--- a/solution.py
+++ b/solution.py
@@ -567,8 +567,38 @@
 )
 
 
-def fit_kernel(regression_ref, sky_ref, flag_ref, weights_ref, out_ref, total_ref):
+def fit_kernel(
+    regression_ref,
+    sky_in,
+    flag_in,
+    weights_in,
+    result_ref,
+    sky_ref,
+    flag_ref,
+    weights_ref,
+    out_ref,
+    total_ref,
+    in_sem,
+    out_sem,
+):
     channels, rows, _ = sky_ref.shape
+    chunks = out_sem.shape[0]
+    size = channels // chunks
+    pairs = ((sky_in, sky_ref), (flag_in, flag_ref), (weights_in, weights_ref))
+    incoming = [
+        [
+            pltpu.make_async_copy(
+                source.at[pl.ds(i * size, size)],
+                target.at[pl.ds(i * size, size)],
+                in_sem.at[k, i],
+            )
+            for k, (source, target) in enumerate(pairs)
+        ]
+        for i in range(chunks)
+    ]
+    for copies in incoming:
+        for copy in copies:
+            copy.start()
 
     def position(channel):
         return (2.0 * channel.astype(jnp.float32) + 1.0) * (1.0 / channels) - 1.0
@@ -594,7 +624,11 @@
         return tuple(powers) + tuple(rights)
 
     zero = jnp.zeros((rows, LANES), jnp.float32)
-    sums = lax.fori_loop(0, channels, gather, (zero,) * 11, unroll=4)
+    sums = (zero,) * 11
+    for i, copies in enumerate(incoming):
+        for copy in copies:
+            copy.wait()
+        sums = lax.fori_loop(i * size, (i + 1) * size, gather, sums, unroll=4)
     powers, rights = sums[:7], sums[7:]
     normal = {}
     for outer in range(4):
@@ -624,21 +658,42 @@
         out_ref[channel] = 0.25 * before + 0.5 * here + 0.25 * after
         return here, after
 
-    before, here = lax.fori_loop(
-        0, channels - 1, smooth, (zero, residual(jnp.int32(0))), unroll=3
-    )
-    out_ref[channels - 1] = 0.25 * before + 0.5 * here
+    state = (zero, residual(jnp.int32(0)))
+    outgoing = []
+    for i in range(chunks):
+        final = i == chunks - 1
+        stop = channels - 1 if final else (i + 1) * size
+        state = lax.fori_loop(i * size, stop, smooth, state, unroll=1 if final else 4)
+        if final:
+            out_ref[channels - 1] = 0.25 * state[0] + 0.5 * state[1]
+        span = pl.ds(i * size, size)
+        outgoing.append(
+            pltpu.make_async_copy(out_ref.at[span], result_ref.at[span], out_sem.at[i])
+        )
+        outgoing[-1].start()
+    for copy in outgoing:
+        copy.wait()
 
 
 def fit(regression, sky, flags, total):
     smem = pl.BlockSpec(memory_space=pltpu.SMEM)
-    vmem = pl.BlockSpec(memory_space=pltpu.VMEM)
+    any_space = pl.BlockSpec(memory_space=pl.ANY)
+    chunks = 8
+    held = pltpu.VMEM(sky.shape, jnp.float32)
     return pl.pallas_call(
         fit_kernel,
-        in_specs=[smem, vmem, vmem, vmem],
-        out_specs=vmem,
+        in_specs=[smem, any_space, any_space, any_space],
+        out_specs=any_space,
         out_shape=jax.ShapeDtypeStruct(sky.shape, jnp.float32),
-        scratch_shapes=[pltpu.VMEM(sky.shape, jnp.float32)],
+        scratch_shapes=[
+            held,
+            pltpu.VMEM(sky.shape, jnp.int32),
+            held,
+            held,
+            held,
+            pltpu.SemaphoreType.DMA((3, chunks)),
+            pltpu.SemaphoreType.DMA((chunks,)),
+        ],
         compiler_params=pltpu.CompilerParams(vmem_limit_bytes=48 << 20),
         name="fit",
     )(regression, sky, flags, total)

time: 196 us -> 195 us (level)
  Pallas kernels: 193 us -> 191 us
where the time goes in v5:
time: 195 us
  Pallas kernels  191 us (98%)
  local copies, waits for them, and re-layouts  3.24 us (2%)
    pallas_call x1, Pallas kernels, exchange(): pl.pallas_call(functools.partial(exchange_kernel, groups=groups, tiles=ti...  178 us
    pallas_call x1, Pallas kernels, fit(): pl.pallas_call(fit_kernel, in_specs=[smem, any_space, any_space, any_spac...  9.55 us

profile of v5, /device:TPU:0, one launch (start us, length us, event | category | flops | bytes accessed | tf_op | source)
XLA Modules:
  0.0 194.6 jit_solution(15642763516189295141)
XLA Ops:
  0.0 1.4 copy.7.offsets_ref
  1.4 3.6 %log_tiles.1.logs_ref = f32[4,9,24,128]{3,2,1,0:T(8,128)} custom-call(s32[1]{0:T(128)} %bitcast.1.where_ref, s32[9,2]{1,0:T(8,128)} %copy.7.offsets_ref, f32[9,128,128]{2,1,0:T(8,128)} %weight_ref.3), custom_call_target="tpu_custom_call" | custom-call | tf_op jit(solution)/shard_map/log_tiles/pallas_call | solution.py:102
  5.0 0.0 copy-start.1
  5.0 178.2 %exchange.1 = (f32[256,24,128]{2,1,0:T(8,128)}, s32[256,24,128]{2,1,0:T(8,128)}, f32[256,24,128]{2,1,0:T(8,128)}) custom-call(s32[9,2]{1,0:T(8,128)} %copy.7.offsets_ref, f32[9,128,128]{2,1,0:T(8,128)} %weight_ref.3, f32[32,9,128,128]{3,2,1,0:T(8,128)} %image_ref.1, s32[32,8,24,128]{3,2,1,0:T(8,128)} %bitcast.2, f32[4,9,24,128]{3,2,1,0:T(8,128)} %log_tiles.1.logs_ref), custom_call_target="tpu_custom_call" | custom-call | tf_op jit(solution)/shard_map/exchange/pallas_call | solution.py:481
  183.1 0.0 copy-done.1
  183.2 0.0 copy-start
  183.2 1.9 copy-done
  185.0 9.6 %fit.1 = f32[256,24,128]{2,1,0:T(8,128)} custom-call(s32[256]{0:T(256)S(1)} %copy-done.1, f32[256,24,128]{2,1,0:T(8,128)S(1)} %copy-done, s32[256,24,128]{2,1,0:T(8,128)} %get-tuple-element.9.flag_in, f32[256,24,128]{2,1,0:T(8,128)} %get-tuple-element.10.weights_in), custom_call_target="tpu_custom_call" | custom-call | tf_op jit(solution)/shard_map/fit/pallas_call | solution.py:683
Async XLA Ops:
  5.0 178.2 %copy-start.1 = (s32[256]{0:T(256)S(1)}, s32[256]{0:T(256)}, u32[]{:S(2)}) copy-start(s32[256]{0:T(256)} %regression_ref.1) | copy-start | bytes 3076
  183.2 1.9 copy-start
